TPU v7x, 32 devices: a whole 2x2x4 slice. The times are simulated.
32 devices in a mesh: dp: 8 (over y, x, core), mp: 4 (over z).
Axes of the slice: x: 2, y: 2, z: 4, core: 2. Of those that a mesh axis runs over, the one named last changes fastest.
Arguments:
- hidden: bfloat16 [1024, 2560], P('dp', 'mp'), may hold values from -6 to 6
- norm_gain: bfloat16 [2560], replicated, may hold values from 0.5 to 1.5
- shared_gate: bfloat16 [2560, 3072], P(None, 'mp'), may hold values from -0.125 to 0.125
- shared_up: bfloat16 [2560, 3072], P(None, 'mp'), may hold values from -0.125 to 0.125
- shared_down: bfloat16 [3072, 2560], P('mp'), may hold values from -0.109375 to 0.109375
- expert_gate: bfloat16 [64, 2560, 1536], P('dp', None, 'mp'), may hold values from -0.125 to 0.125
- expert_up: bfloat16 [64, 2560, 1536], P('dp', None, 'mp'), may hold values from -0.125 to 0.125
- expert_down: bfloat16 [64, 1536, 2560], P('dp', 'mp'), may hold values from -0.15625 to 0.15625
- adapter_in: bfloat16 [64, 3072, 16], P('dp', 'mp'), may hold values from -0.109375 to 0.109375
- adapter_out: bfloat16 [64, 16, 2560], P('dp'), may hold values from -1.5 to 1.5
- active: int32 [16], replicated, may hold values from 0 to 63, as said below
- lengths: int32 [64], replicated, may hold values from 1 to 256, 1024 in all
- request_adapter: int32 [64], replicated, may hold values from 0 to 15
- routes: int32 [1024, 6], P('dp'), may hold values from 0 to 63, all different within a row; in each aligned block of 128 rows (0 to 127, 128 to 255, ...) at most 16 rows name the same one
- route_weights: float32 [1024, 6], P('dp'), may hold values from 0.05 to 0.35
Outputs:
- layer_out: bfloat16 [1024, 2560], P('dp', 'mp')
Inputs may be any that keep to these rules, and one draw needn't show every extreme that they name: `active`: the entries are distinct. `routes`: within the 128 rows of one index of dp no expert is named more than 16 times, and that many is reached; a row names distinct experts.
All inputs are finite; a program needn't handle non-finite values.
Results may differ from a plain program's by a relative error of at most 0.015.
Values may be sent and summed in bfloat16 or wider, within the bound.
A program may use at most 128 MiB of HBM per device.

v0:
```python
import jax
import jax.numpy as jnp
from jax import lax
from jax.sharding import PartitionSpec as P

F32 = jnp.float32
BF16 = jnp.bfloat16


def body(
    hidden,
    norm_gain,
    shared_gate,
    shared_up,
    shared_down,
    expert_gate,
    expert_up,
    expert_down,
    adapter_in,
    adapter_out,
    active,
    lengths,
    request_adapter,
    routes,
    route_weights,
):
    rows, top = routes.shape
    dp = lax.axis_size("dp")
    mp = lax.axis_size("mp")
    me = lax.axis_index("dp")
    experts = expert_gate.shape[0]
    cap = mp * max(1, rows * top * 4 // (experts * dp * mp * 3))
    tokens = rows * dp
    table = jnp.concatenate([routes.astype(F32), route_weights], axis=1)
    table = lax.all_gather(table, "dp", axis=0, tiled=True)
    gathered = lax.all_gather(hidden, "mp", axis=1, tiled=True)
    values = gathered.astype(F32)
    factor = lax.rsqrt(jnp.mean(values * values, axis=-1, keepdims=True) + 1e-06)
    own_normed = (values * factor * norm_gain.astype(F32)).astype(BF16)
    normed = lax.all_gather(own_normed, "dp", axis=0, tiled=True)
    width = normed.shape[1]

    all_routes = table[:, :top].reshape(dp, rows, top)
    all_weights = table[:, top:].reshape(dp, rows, top)
    local = (me * experts + jnp.arange(experts, dtype=jnp.int32)).astype(F32)
    match = all_routes[..., None] == local
    hits = jnp.sum(match.astype(F32), axis=2)
    weight = jnp.sum(jnp.where(match, all_weights[..., None], 0.0), axis=2)
    lower = (jnp.arange(rows)[:, None] > jnp.arange(rows)[None, :]).astype(BF16)
    place = jnp.einsum("ut,stj->suj", lower, hits.astype(BF16), preferred_element_type=F32)
    place = jnp.where(hits > 0.5, place, -1.0)
    pick = place[..., None] == jnp.arange(cap, dtype=F32)
    slot_weight = jnp.sum(jnp.where(pick, weight[..., None], 0.0), axis=1)
    pick = pick.astype(BF16)

    slots_in = jnp.einsum("stjc,std->jscd", pick, normed.reshape(dp, rows, width), preferred_element_type=F32)
    slots_in = slots_in.astype(BF16).reshape(experts, dp * cap, width)
    gate_val = jnp.einsum("jcd,jdf->jcf", slots_in, expert_gate, preferred_element_type=F32)
    up_val = jnp.einsum("jcd,jdf->jcf", slots_in, expert_up, preferred_element_type=F32)
    inner = (jax.nn.silu(gate_val) * up_val).astype(BF16)
    result = jnp.einsum("jcf,jfd->jcd", inner, expert_down, preferred_element_type=F32)
    result = result.reshape(experts, dp, cap, width) * jnp.transpose(slot_weight, (1, 0, 2))[..., None]
    routed = jnp.einsum("stjc,jscd->std", pick, result.astype(BF16), preferred_element_type=F32)

    shared_lin = jnp.dot(normed, shared_gate, preferred_element_type=F32)
    shared_pre = jnp.dot(normed, shared_up, preferred_element_type=F32)
    shared_act = (jax.nn.silu(shared_lin) * shared_pre).astype(BF16)

    adapters, _, rank = adapter_in.shape
    request_end = jnp.cumsum(lengths)
    request_start = request_end - lengths
    positions = jnp.arange(tokens, dtype=jnp.int32)[:, None]
    inside = (positions >= request_start[None, :]) & (positions < request_end[None, :])
    pool_id = jnp.sum(
        jnp.where(request_adapter[:, None] == jnp.arange(active.shape[0])[None, :], active[None, :], 0), axis=1
    )
    adapter_of = jnp.sum(jnp.where(inside, pool_id[None, :], 0), axis=1)
    owned = me * adapters + jnp.arange(adapters * rank, dtype=jnp.int32) // rank
    chosen = adapter_of[:, None] == owned[None, :]
    in_matrix = jnp.transpose(adapter_in, (1, 0, 2)).reshape(shared_act.shape[1], adapters * rank)
    lowrank = jnp.dot(shared_act, in_matrix, preferred_element_type=F32)
    lowrank = jnp.where(chosen, lowrank, 0.0)
    high = lowrank.astype(BF16)
    adapted = jnp.dot(high, adapter_out.reshape(adapters * rank, width), preferred_element_type=F32)

    own_act = lax.dynamic_slice_in_dim(shared_act, me * rows, rows, axis=0)
    own_shared = jnp.dot(own_act, shared_down, preferred_element_type=F32)
    is_own = (jnp.arange(dp) == me)[:, None, None]
    total = routed + adapted.reshape(dp, rows, width) + jnp.where(is_own, own_shared[None], 0.0)
    total = total.astype(BF16).reshape(tokens, width)
    part = lax.psum_scatter(total, "dp", scatter_dimension=0, tiled=True)
    return lax.psum_scatter(part, "mp", scatter_dimension=1, tiled=True)


def solution(mesh):
    in_specs = (
        P("dp", "mp"),
        P(),
        P(None, "mp"),
        P(None, "mp"),
        P("mp", None),
        P("dp", None, "mp"),
        P("dp", None, "mp"),
        P("dp", "mp", None),
        P("dp", "mp", None),
        P("dp", None, None),
        P(),
        P(),
        P(),
        P("dp", None),
        P("dp", None),
    )
    return jax.shard_map(body, mesh=mesh, in_specs=in_specs, out_specs=P("dp", "mp"), check_vma=False)
```

profile of v0, /device:TPU:0, one launch (start us, length us, event | category | flops | bytes accessed | tf_op | source)
XLA Modules:
  0.0 219.8 jit_solution(10707472512558185167)
XLA Ops:
  6.5 0.8 convert_element_type.53
  7.3 19.8 %all_gather.10 = bf16[128,2560]{1,0:T(8,128)(2,1)S(1)} all-gather(bf16[128,640]{1,0:T(8,128)(2,1)} %param.15), channel_id=1, replica_groups=mesh['dp'=8,'mp'=4] {'mp'}, dimensions={1}, use_global_device_ids=true | all-gather | bytes 819200 | tf_op jit(solution)/shard_map/all_gather | solution.py:36
  27.1 0.2 fusion.6
  27.4 1.1 fusion.8
  28.4 0.0 all-gather.2.cloned.1.call-update
  28.5 0.0 reduce-scatter.5.cloned.1.call-start
  28.5 0.7 convert_element_type.48
  29.2 0.7 copy.34
  29.9 0.1 reduce-window.8
  30.0 0.1 reduce
  30.2 0.7 sub.9
  30.8 0.7 pad_maximum_fusion
  31.5 9.2 %all_gather.9 = f32[1024,12]{0,1:T(8,128)S(1)} all-gather(f32[128,12]{0,1:T(8,128)S(1)} %pad_maximum_fusion), channel_id=1, replica_groups=mesh['dp'=8,'mp'=4] {'dp'}, dimensions={0}, use_global_device_ids=true | all-gather | bytes 55296 | tf_op jit(solution)/shard_map/all_gather | solution.py:35
  40.7 0.8 select_reduce_fusion.2
  41.5 0.1 fusion.14
  41.6 0.1 select_reduce_fusion.1
  41.7 0.1 fusion.10
  41.9 0.2 select_reduce_fusion
  42.1 0.1 iota_compare_fusion
  42.2 27.8 %all-gather.2.cloned.1.call-done = bf16[1024,2560]{1,0:T(8,128)(2,1)} async-done(((bf16[128,2560]{1,0:T(8,128)(2,1)}), bf16[1024,2560]{1,0:T(8,128)(2,1)}) %all-gather.2.cloned.1.call-update) | async-done | bytes 5242896 | tf_op jit(solution)/shard_map/all_gather | solution.py:40
  70.0 4.0 %fusion.22 = f32[8,2560,128]{1,2,0:S(1)} fusion(bf16[8,128,2560]{2,1,0:T(8,128)(2,1)} %bitcast.68, pred[8,128,128]{1,2,0:T(8,128)(4,1)S(1)} %bitcast.72), kind=kOutput, calls=%fused_computation.49 | convolution fusion | flops 671088640 | bytes 15859712
  74.0 3.1 %convert_bitcast_fusion = bf16[8,8,16,2560]{3,2,0,1:T(8,128)(2,1)} fusion(f32[8,2560,8,16]{1,3,2,0:T(8,128)S(1)} %bitcast.66), kind=kLoop, calls=%fused_computation.7 | loop fusion | flops 2621440 | bytes 15728640 | tf_op jit(solution)/shard_map/convert_element_type | solution.py:57
  77.1 2.8 %copy.31 = bf16[8,8,16,2560]{3,2,1,0:T(8,128)(2,1)S(1)} copy(bf16[8,8,16,2560]{3,2,0,1:T(8,128)(2,1)} %convert_bitcast_fusion) | data formatting | bytes 10485760 | tf_op jit(solution)/shard_map/convert_element_type | solution.py:57
  79.9 2.2 %copy-done.1 = bf16[8,8,16,2560]{3,2,1,0:T(8,128)(2,1)} copy-done((bf16[8,8,16,2560]{3,2,1,0:T(8,128)(2,1)}, bf16[8,8,16,2560]{3,2,1,0:T(8,128)(2,1)S(1)}, u32[]{:S(2)}) %copy-start.1) | copy-done | bytes 5242904
  82.2 7.1 %fusion.23 = f32[8,128,384]{2,1,0:T(8,128)S(1)} fusion(bf16[8,128,2560]{2,1,0:T(8,128)(2,1)S(1)} %bitcast.64, bf16[8,2560,384]{2,1,0:T(8,128)(2,1)} %param.20), kind=kOutput, calls=%fused_computation.50 | convolution fusion | flops 2013265920 | bytes 22544384 | tf_op jit(solution)/shard_map/jcd,jdf->jcf/dot_general | solution.py:58
  89.3 0.0 slice-start
  89.3 18.8 %fusion.24 = f32[8,128,2560]{2,1,0:T(8,128)} fusion(bf16[8,384,2560]{2,1,0:T(8,128)(2,1)} %param.22, f32[8,128,384]{2,1,0:T(8,128)S(1)} %fusion.23, bf16[8,128,2560]{2,1,0:T(8,128)(2,1)} %bitcast.65, bf16[8,2560,384]{2,1,0:T(8,128)(2,1)} %param.21), kind=kOutput, calls=%fused_computation.51 | convolution fusion | flops 4028891136 | bytes 48758784 | tf_op jit(solution)/shard_map/jcf,jfd->jcd/dot_general | solution.py:61
  108.2 5.7 %fusion.3 = f32[8,128,2560,1]{2,1,3,0:T(8,128)S(1)} fusion(f32[8,8,16,2560]{3,2,1,0:T(8,128)} %bitcast.63, f32[8,8,16]{2,0,1:T(8,128)S(1)} %bitcast.74, f32[8,128,8]{1,2,0:T(8,128)S(1)} %fusion.10), kind=kOutput, calls=%fused_computation.5 | convolution fusion | flops 676462592 | bytes 21008384 | tf_op jit(solution)/shard_map/stjc,jscd->std/dot_general | solution.py:63
  113.9 0.0 copy-done.3
  113.9 0.0 copy-start.4
  113.9 6.5 %fusion.25 = f32[1024,768]{1,0:T(8,128)S(1)} fusion(bf16[1024,2560]{1,0:T(8,128)(2,1)} %all-gather.2.cloned.1.call-done, bf16[2560,768]{1,0:T(8,128)(2,1)S(1)} %copy-done.3), kind=kOutput, calls=%fused_computation.52 | convolution fusion | flops 4026531840 | bytes 12320768 | tf_op jit(solution)/shard_map/dot_general | solution.py:65
  120.4 0.0 slice-done
  120.4 0.0 slice-done.1
  120.4 0.0 copy-done.4
  120.4 0.0 copy-start.2
  120.4 4.4 %multiply_convert_fusion = bf16[1024,768]{1,0:T(8,128)(2,1)S(1)} fusion(f32[1024,768]{1,0:T(8,128)S(1)} %fusion.25, bf16[1024,2560]{1,0:T(8,128)(2,1)S(1)} %bitcast.70, bf16[2560,768]{1,0:T(8,128)(2,1)S(1)} %copy-done.4), kind=kOutput, calls=%fused_computation.8 | convolution fusion | flops 4031250432 | bytes 13893632 | tf_op jit(solution)/shard_map/dot_general | solution.py:66
  124.9 0.0 copy-start.5
  124.9 0.7 fusion.15
  125.6 0.2 copy-done.5
  125.8 0.6 fusion.9
  126.4 3.8 %fusion.1 = bf16[8,128,2560]{2,1,0:T(8,128)(2,1)} fusion(f32[8,128,2560,1]{2,1,3,0:T(8,128)S(1)} %fusion.3, bf16[8,128,128]{2,1,0:T(8,128)(2,1)S(1)} %bitcast.73, bf16[128,2560,1]{1,0,2:T(8,128)(2,1)S(1)} %bitcast.62, f32[128,2560]{1,0:T(8,128)S(1)} %fusion.15, pred[8]{0:T(512)(128)(4,1)S(1)} %iota_compare_fusion.6), kind=kOutput, calls=%fused_computation.2 | convolution fusion | flops 681574400 | bytes 17956872 | tf_op jit(solution)/shard_map/dot_general | solution.py:84
  130.2 0.0 reduce-scatter.5.cloned.1.call-update
  130.3 0.0 reduce-scatter.7.cloned.1.call-start
  130.3 56.7 %reduce-scatter.5.cloned.1.call-done = bf16[128,2560]{1,0:T(8,128)(2,1)} async-done(((bf16[1024,2560]{1,0:T(8,128)(2,1)}), bf16[128,2560]{1,0:T(8,128)(2,1)}) %reduce-scatter.5.cloned.1.call-update) | async-done | bytes 655376 | tf_op jit(solution)/shard_map/reduce_scatter | solution.py:91
  187.0 2.2 copy.36
  189.1 0.0 reduce-scatter.7.cloned.1.call-update
  189.2 22.4 %reduce-scatter.7.cloned.1.call-done = bf16[640,128]{1,0:T(8,128)(2,1)} async-done(((bf16[2560,128]{1,0:T(8,128)(2,1)}), bf16[640,128]{1,0:T(8,128)(2,1)}) %reduce-scatter.7.cloned.1.call-update) | async-done | bytes 163856
  211.6 1.7 copy.37
  (13 shorter events, 0.0 us)
Async XLA Ops:
  6.5 119.9 %copy-start = (bf16[8,16,2560]{2,1,0:T(8,128)(2,1)S(1)}, bf16[8,16,2560]{2,1,0:T(8,128)(2,1)}, u32[]{:S(2)}) copy-start(bf16[8,16,2560]{2,1,0:T(8,128)(2,1)} %param.24) | copy-start | bytes 1966084
  6.5 63.5 %all-gather.2.cloned.1.call-start = ((), (), s32[]{:S(2)}) async-start(), calls=%async_computation.2 | async-start | bytes 5898240 | tf_op jit(solution)/shard_map/all_gather | solution.py:40
  28.5 158.5 %reduce-scatter.5.cloned.1.call-start = ((), (), s32[]{:S(2)}) async-start(), calls=%async_computation.3 | async-start | bytes 5898240 | tf_op jit(solution)/shard_map/reduce_scatter | solution.py:91
  79.9 2.2 %copy-start.1 = (bf16[8,8,16,2560]{3,2,1,0:T(8,128)(2,1)}, bf16[8,8,16,2560]{3,2,1,0:T(8,128)(2,1)S(1)}, u32[]{:S(2)}) copy-start(bf16[8,8,16,2560]{3,2,1,0:T(8,128)(2,1)S(1)} %copy.31) | copy-start | bytes 15728644
  89.3 31.1 %slice-start = ((s8[5242880]{0:T(1024)(128)(4,1)}), s8[1048576]{0:T(1024)(128)(4,1)S(1)}, s32[]{:S(2)}) async-start(s8[5242880]{0:T(1024)(128)(4,1)} %bitcast.69), calls=%async_computation.5 | async-start | bytes 2097152
  108.1 5.7 %copy-start.3 = (bf16[2560,768]{1,0:T(8,128)(2,1)S(1)}, bf16[2560,768]{1,0:T(8,128)(2,1)}, u32[]{:S(2)}) copy-start(bf16[2560,768]{1,0:T(8,128)(2,1)} %param.17) | copy-start | bytes 11796484
  108.2 12.3 %slice-start.1 = ((s8[5242880]{0:T(1024)(128)(4,1)}), s8[4194304]{0:T(1024)(128)(4,1)S(1)}, s32[]{:S(2)}) async-start(s8[5242880]{0:T(1024)(128)(4,1)} %bitcast.69), calls=%async_computation.6 | async-start | bytes 8388608
  113.9 6.5 %copy-start.4 = (bf16[2560,768]{1,0:T(8,128)(2,1)S(1)}, bf16[2560,768]{1,0:T(8,128)(2,1)}, u32[]{:S(2)}) copy-start(bf16[2560,768]{1,0:T(8,128)(2,1)} %param.18) | copy-start | bytes 11796484
  120.4 4.5 %copy-start.2 = (bf16[768,2560]{1,0:T(8,128)(2,1)S(1)}, bf16[768,2560]{1,0:T(8,128)(2,1)}, u32[]{:S(2)}) copy-start(bf16[768,2560]{1,0:T(8,128)(2,1)} %param.19) | copy-start | bytes 11796484
  124.9 0.9 copy-start.5
  130.3 81.3 %reduce-scatter.7.cloned.1.call-start = ((), (), s32[]{:S(2)}) async-start(), calls=%async_computation.4 | async-start | bytes 819200
Sparse Core Ops, SparseCore 0:
  28.6 41.3 all-gather.1
  130.4 56.5 reduce-scatter.4
  189.4 22.1 reduce-scatter.6
where the time goes:
time: 220 us
  waiting for transfers between devices  107 us (49%)
  matrix products  51.8 us (24%)
  blocking collectives  29.1 us (13%)
  between operations  13.3 us (6%)
  local copies, waits for them, and re-layouts  9.94 us (5%)
  other arithmetic  8.73 us (4%)
    reduce_scatter x1, waiting for transfers between devices, body(): part = lax.psum_scatter(total, 'dp', scatter_dimension=0, tiled=True)  56.7 us
    all_gather x1, waiting for transfers between devices, body(): normed = lax.all_gather(own_normed, 'dp', axis=0, tiled=True)  27.8 us
    unnamed x4, waiting for transfers between devices  22.4 us
    all_gather x1, blocking collectives, body(): gathered = lax.all_gather(hidden, 'mp', axis=1, tiled=True)  19.8 us
    dot_general x1, matrix products, body(): jnp.einsum('jcf,jfd->jcd', inner, expert_down, preferred_element_type=F32)  18.8 us
    all_gather x1, blocking collectives, body(): table = lax.all_gather(table, 'dp', axis=0, tiled=True)  9.21 us
    dot_general x1, matrix products, body(): jnp.einsum('jcd,jdf->jcf', slots_in, expert_gate, preferred_element_type=...  7.14 us
    dot_general x1, matrix products, body(): shared_lin = jnp.dot(normed, shared_gate, preferred_element_type=F32)  6.48 us
  transfers between devices with their start and end apart: 3, of which 3 were waited for; matrix products, arithmetic and copies ran while one was open for 2% of the time, Pallas kernels for 0%

commit v1 on v0

--- a/solution.py
+++ b/solution.py
@@ -1,10 +1,118 @@
+import functools
+
 import jax
 import jax.numpy as jnp
 from jax import lax
+from jax.experimental import pallas as pl
+from jax.experimental.pallas import tpu as pltpu
 from jax.sharding import PartitionSpec as P
 
 F32 = jnp.float32
 BF16 = jnp.bfloat16
+
+
+MESH = pl.DeviceIdType.MESH
+
+
+def other(me, bits):
+    for bit in (1, 2, 4):
+        if bits & bit:
+            me = me + bit - 2 * bit * ((me // bit) % 2)
+    return me
+
+
+def greet(me, z, mp):
+    barrier = pltpu.get_barrier_semaphore()
+    for flip in (1, 2, 4):
+        pl.semaphore_signal(barrier, inc=1, device_id={"dp": other(me, flip), "mp": z}, device_id_type=MESH)
+    for k in range(1, mp):
+        pl.semaphore_signal(barrier, inc=1, device_id={"dp": me, "mp": lax.rem(z + k, mp)}, device_id_type=MESH)
+    pl.semaphore_wait(barrier, 3 + mp - 1)
+
+
+def scatter_kernel(mp, total, out, near, first, second, final, parts, send_sem, recv_sem):
+    me = lax.axis_index("dp")
+    z = lax.axis_index("mp")
+    width = total.shape[2]
+    half = width // 2
+    part = width // mp
+    sides = (pl.ds(0, half), pl.ds(half, half))
+    greet(me, z, mp)
+
+    def send(src, dst, number, dp_to, mp_to):
+        copy = pltpu.make_async_remote_copy(
+            src_ref=src,
+            dst_ref=dst,
+            send_sem=send_sem.at[number],
+            recv_sem=recv_sem.at[number],
+            device_id={"dp": dp_to, "mp": mp_to},
+            device_id_type=MESH,
+        )
+        copy.start()
+        return copy
+
+    order = (3, 1, 2, 0)
+    near_copies = {r: send(total.at[other(me, 2 * r + 1)], near.at[r], r, other(me, 1), z) for r in order}
+    flips = ((1, 2), (2, 1))
+    first_copies = {}
+    for r in order:
+        near_copies[r].wait_recv()
+        near[r] = (near[r].astype(F32) + total[other(me, 2 * r)].astype(F32)).astype(BF16)
+        for side in range(2):
+            one, two = flips[side]
+            if r & one:
+                late = 0 if r & two else 1
+                first_copies[side, late] = send(
+                    near.at[r, :, sides[side]], first.at[side, late], 4 + 2 * side + late, other(me, 2 * one), z
+                )
+    second_copies = []
+    for side in range(2):
+        one, two = flips[side]
+        first_copies[side, 0].wait_recv()
+        first[side, 0] = (first[side, 0].astype(F32) + near[two, :, sides[side]].astype(F32)).astype(BF16)
+        second_copies.append(send(first.at[side, 0], second.at[side], 8 + side, other(me, 2 * two), z))
+    for side in range(2):
+        first_copies[side, 1].wait_recv()
+        second_copies[side].wait_recv()
+        whole = (
+            near[0, :, sides[side]].astype(F32) + first[side, 1].astype(F32) + second[side].astype(F32)
+        ).astype(BF16)
+        for m in range(mp // 2):
+            final[side * (mp // 2) + m] = whole[:, m * part : (m + 1) * part]
+    part_copies = []
+    for k in (2, 1, 3):
+        to = lax.rem(z + k, mp)
+        part_copies.append(send(final.at[to], parts.at[k - 1], 10 + k - 1, me, to))
+    result = final[z].astype(F32)
+    for copy, k in zip(part_copies, (2, 1, 3)):
+        copy.wait_recv()
+        result = result + parts[k - 1].astype(F32)
+    out[...] = result.astype(BF16)
+    for copy in [*near_copies.values(), *first_copies.values(), *second_copies, *part_copies]:
+        copy.wait_send()
+
+
+def reduce_scatter(total, mp):
+    dp, rows, width = total.shape
+    half = width // 2
+    copies = 10 + mp - 1
+    vmem = pl.BlockSpec(memory_space=pltpu.VMEM)
+    return pl.pallas_call(
+        functools.partial(scatter_kernel, mp),
+        out_shape=jax.ShapeDtypeStruct((rows, width // mp), BF16),
+        in_specs=[vmem],
+        out_specs=vmem,
+        scratch_shapes=[
+            pltpu.VMEM((4, rows, width), BF16),
+            pltpu.VMEM((2, 2, rows, half), BF16),
+            pltpu.VMEM((2, rows, half), BF16),
+            pltpu.VMEM((mp, rows, width // mp), BF16),
+            pltpu.VMEM((mp - 1, rows, width // mp), BF16),
+            pltpu.SemaphoreType.DMA((copies,)),
+            pltpu.SemaphoreType.DMA((copies,)),
+        ],
+        compiler_params=pltpu.CompilerParams(collective_id=0, has_side_effects=True, vmem_limit_bytes=40 * 2**20),
+    )(total)
 
 
 def body(
@@ -87,7 +195,10 @@
     own_shared = jnp.dot(own_act, shared_down, preferred_element_type=F32)
     is_own = (jnp.arange(dp) == me)[:, None, None]
     total = routed + adapted.reshape(dp, rows, width) + jnp.where(is_own, own_shared[None], 0.0)
-    total = total.astype(BF16).reshape(tokens, width)
+    total = total.astype(BF16)
+    if dp == 8 and mp == 4:
+        return reduce_scatter(total, mp)
+    total = total.reshape(tokens, width)
     part = lax.psum_scatter(total, "dp", scatter_dimension=0, tiled=True)
     return lax.psum_scatter(part, "mp", scatter_dimension=1, tiled=True)
 

time: 220 us -> 178 us (0.81)
  waiting for transfers between devices: 107 us -> 27.8 us
  Pallas kernels: 0 us -> 41.6 us
  local copies, waits for them, and re-layouts: 9.94 us -> 6.74 us
  matrix products: 51.8 us -> 49.5 us
    reduce_scatter x1 -> x0, waiting for transfers between devices: 56.7 us -> none  [body(): part = lax.psum_scatter(total, 'dp', scatter_dimension=0, tiled=True)]
    pallas_call x0 -> x1, Pallas kernels: none -> 41.6 us  [reduce_scatter(): pl.pallas_call(functools.partial(scatter_kernel, mp), out_shape=jax.Shape...]
    unnamed x4 -> x1, waiting for transfers between devices: 22.4 us -> 0.02 us
    unnamed x18 -> x17, local copies, waits for them, and re-layouts: 6.37 us -> 3.16 us
    dot_general x1, matrix products: 3.84 us -> 1.52 us  [body(): jnp.dot(high, adapter_out.reshape(adapters * rank, width), preferred_elem...]
  transfers between devices with their start and end apart: 3 -> 1, of which waited for: 3 -> 1; matrix products, arithmetic and copies ran while one was open for 2% -> 3% of each run, Pallas kernels for 0% -> 0%
where the time goes in v1:
time: 178 us; the launch traced here: 177 us
  matrix products  49.5 us (28%)
  Pallas kernels  41.6 us (23%)
  blocking collectives  29.1 us (16%)
  waiting for transfers between devices  27.8 us (16%)
  between operations  13.6 us (8%)
  other arithmetic  8.73 us (5%)
  local copies, waits for them, and re-layouts  6.74 us (4%)
    pallas_call x1, Pallas kernels, reduce_scatter(): pl.pallas_call(functools.partial(scatter_kernel, mp), out_shape=jax.Shape...  41.6 us
    all_gather x1, waiting for transfers between devices, body(): normed = lax.all_gather(own_normed, 'dp', axis=0, tiled=True)  27.8 us
    all_gather x1, blocking collectives, body(): gathered = lax.all_gather(hidden, 'mp', axis=1, tiled=True)  19.8 us
    dot_general x1, matrix products, body(): jnp.einsum('jcf,jfd->jcd', inner, expert_down, preferred_element_type=F32)  18.8 us
    all_gather x1, blocking collectives, body(): table = lax.all_gather(table, 'dp', axis=0, tiled=True)  9.21 us
    dot_general x1, matrix products, body(): jnp.einsum('jcd,jdf->jcf', slots_in, expert_gate, preferred_element_type=...  7.14 us
    dot_general x1, matrix products, body(): shared_lin = jnp.dot(normed, shared_gate, preferred_element_type=F32)  6.48 us
    dot_general x1, matrix products, body(): jnp.einsum('stjc,jscd->std', pick, result.astype(BF16), preferred_element...  5.73 us
  transfers between devices with their start and end apart: 1, of which 1 were waited for; matrix products, arithmetic and copies ran while one was open for 3% of the time, Pallas kernels for 0%

profile of v1, /device:TPU:0, one launch (start us, length us, event | category | flops | bytes accessed | tf_op | source)
XLA Modules:
  0.0 177.1 jit_solution(2674006047006978663)
XLA Ops:
  6.5 0.0 copy-start
  6.5 0.0 all-gather.2.cloned.1.call-start
  6.5 0.8 convert_element_type.53
  7.3 19.8 %all_gather.10 = bf16[128,2560]{1,0:T(8,128)(2,1)S(1)} all-gather(bf16[128,640]{1,0:T(8,128)(2,1)} %param.15), channel_id=1, replica_groups=mesh['dp'=8,'mp'=4] {'mp'}, dimensions={1}, use_global_device_ids=true | all-gather | bytes 819200 | tf_op jit(solution)/shard_map/all_gather | solution.py:144
  27.1 0.2 fusion.6
  27.4 1.1 fusion.8
  28.4 0.0 all-gather.2.cloned.1.call-update
  28.5 0.7 convert_element_type.48
  29.2 0.7 copy.29
  29.9 0.1 reduce-window.8
  30.0 0.1 reduce
  30.1 0.7 sub.9
  30.8 0.7 pad_maximum_fusion
  31.5 9.2 %all_gather.9 = f32[1024,12]{0,1:T(8,128)S(1)} all-gather(f32[128,12]{0,1:T(8,128)S(1)} %pad_maximum_fusion), channel_id=1, replica_groups=mesh['dp'=8,'mp'=4] {'dp'}, dimensions={0}, use_global_device_ids=true | all-gather | bytes 55296 | tf_op jit(solution)/shard_map/all_gather | solution.py:143
  40.7 0.8 select_reduce_fusion.2
  41.5 0.1 fusion.14
  41.6 0.1 select_reduce_fusion.1
  41.7 0.1 fusion.10
  41.8 0.2 select_reduce_fusion
  42.1 0.1 iota_compare_fusion
  42.2 27.8 %all-gather.2.cloned.1.call-done = bf16[1024,2560]{1,0:T(8,128)(2,1)} async-done(((bf16[128,2560]{1,0:T(8,128)(2,1)}), bf16[1024,2560]{1,0:T(8,128)(2,1)}) %all-gather.2.cloned.1.call-update) | async-done | bytes 5242896 | tf_op jit(solution)/shard_map/all_gather | solution.py:148
  70.0 4.0 %fusion.22 = f32[8,2560,128]{1,2,0:S(1)} fusion(bf16[8,128,2560]{2,1,0:T(8,128)(2,1)} %bitcast.64, pred[8,128,128]{1,2,0:T(8,128)(4,1)S(1)} %bitcast.67), kind=kOutput, calls=%fused_computation.49 | convolution fusion | flops 671088640 | bytes 15859712
  73.9 3.1 %convert_bitcast_fusion = bf16[8,8,16,2560]{3,2,0,1:T(8,128)(2,1)} fusion(f32[8,2560,8,16]{1,3,2,0:T(8,128)S(1)} %bitcast.63), kind=kLoop, calls=%fused_computation.7 | loop fusion | flops 2621440 | bytes 15728640 | tf_op jit(solution)/shard_map/convert_element_type | solution.py:165
  77.1 2.8 %copy.26 = bf16[8,8,16,2560]{3,2,1,0:T(8,128)(2,1)S(1)} copy(bf16[8,8,16,2560]{3,2,0,1:T(8,128)(2,1)} %convert_bitcast_fusion) | data formatting | bytes 10485760 | tf_op jit(solution)/shard_map/convert_element_type | solution.py:165
  79.9 0.0 copy-start.1
  79.9 2.2 %copy-done.1 = bf16[8,8,16,2560]{3,2,1,0:T(8,128)(2,1)} copy-done((bf16[8,8,16,2560]{3,2,1,0:T(8,128)(2,1)}, bf16[8,8,16,2560]{3,2,1,0:T(8,128)(2,1)S(1)}, u32[]{:S(2)}) %copy-start.1) | copy-done | bytes 5242904
  82.1 7.1 %fusion.23 = f32[8,128,384]{2,1,0:T(8,128)S(1)} fusion(bf16[8,128,2560]{2,1,0:T(8,128)(2,1)S(1)} %bitcast.61, bf16[8,2560,384]{2,1,0:T(8,128)(2,1)} %param.20), kind=kOutput, calls=%fused_computation.50 | convolution fusion | flops 2013265920 | bytes 22544384 | tf_op jit(solution)/shard_map/jcd,jdf->jcf/dot_general | solution.py:166
  89.3 0.0 slice-start
  89.3 18.8 %fusion.24 = f32[8,128,2560]{2,1,0:T(8,128)} fusion(bf16[8,384,2560]{2,1,0:T(8,128)(2,1)} %param.22, f32[8,128,384]{2,1,0:T(8,128)S(1)} %fusion.23, bf16[8,128,2560]{2,1,0:T(8,128)(2,1)} %bitcast.62, bf16[8,2560,384]{2,1,0:T(8,128)(2,1)} %param.21), kind=kOutput, calls=%fused_computation.51 | convolution fusion | flops 4028891136 | bytes 48758784 | tf_op jit(solution)/shard_map/jcf,jfd->jcd/dot_general | solution.py:169
  108.1 0.0 copy-start.3
  108.1 5.7 %fusion.3 = f32[8,128,2560,1]{2,1,3,0:T(8,128)S(1)} fusion(f32[8,8,16,2560]{3,2,1,0:T(8,128)} %bitcast.60, f32[8,8,16]{2,0,1:T(8,128)S(1)} %bitcast.69, f32[8,128,8]{1,2,0:T(8,128)S(1)} %fusion.10), kind=kOutput, calls=%fused_computation.5 | convolution fusion | flops 676462592 | bytes 21008384 | tf_op jit(solution)/shard_map/stjc,jscd->std/dot_general | solution.py:171
  113.8 0.0 copy-done.3
  113.8 0.0 copy-start.4
  113.9 6.5 %fusion.25 = f32[1024,768]{1,0:T(8,128)S(1)} fusion(bf16[1024,2560]{1,0:T(8,128)(2,1)} %all-gather.2.cloned.1.call-done, bf16[2560,768]{1,0:T(8,128)(2,1)S(1)} %copy-done.3), kind=kOutput, calls=%fused_computation.52 | convolution fusion | flops 4026531840 | bytes 12320768 | tf_op jit(solution)/shard_map/dot_general | solution.py:173
  120.3 0.0 slice-done
  120.4 0.0 slice-done.1
  120.4 0.0 copy-done.4
  120.4 0.0 copy-start.2
  120.4 4.5 %multiply_convert_fusion = bf16[1024,768]{1,0:T(8,128)(2,1)S(1)} fusion(f32[1024,768]{1,0:T(8,128)S(1)} %fusion.25, bf16[1024,2560]{1,0:T(8,128)(2,1)S(1)} %bitcast.66, bf16[2560,768]{1,0:T(8,128)(2,1)S(1)} %copy-done.4), kind=kOutput, calls=%fused_computation.8 | convolution fusion | flops 4031250432 | bytes 13893632 | tf_op jit(solution)/shard_map/dot_general | solution.py:174
  124.9 0.0 copy-done.2
  124.9 0.0 copy-start.5
  124.9 0.7 fusion.15
  125.6 0.2 copy-done.5
  125.8 0.6 fusion.9
  126.4 0.0 copy-done
  126.4 1.5 fusion.1.total
  127.9 41.6 %shard_map.145 = bf16[128,640]{1,0:T(8,128)(2,1)S(1)} custom-call(bf16[8,128,2560]{2,1,0:T(8,128)(2,1)S(1)} %fusion.1.total), custom_call_target="tpu_custom_call" | custom-call | tf_op jit(solution)/shard_map/pallas_call | solution.py:100
  169.6 0.7 copy.36
  (7 shorter events, 0.0 us)
Async XLA Ops:
  6.5 119.9 %copy-start = (bf16[8,16,2560]{2,1,0:T(8,128)(2,1)S(1)}, bf16[8,16,2560]{2,1,0:T(8,128)(2,1)}, u32[]{:S(2)}) copy-start(bf16[8,16,2560]{2,1,0:T(8,128)(2,1)} %param.24) | copy-start | bytes 1966084
  6.5 63.4 %all-gather.2.cloned.1.call-start = ((), (), s32[]{:S(2)}) async-start(), calls=%async_computation | async-start | bytes 5898240 | tf_op jit(solution)/shard_map/all_gather | solution.py:148
  79.9 2.2 %copy-start.1 = (bf16[8,8,16,2560]{3,2,1,0:T(8,128)(2,1)}, bf16[8,8,16,2560]{3,2,1,0:T(8,128)(2,1)S(1)}, u32[]{:S(2)}) copy-start(bf16[8,8,16,2560]{3,2,1,0:T(8,128)(2,1)S(1)} %copy.26) | copy-start | bytes 15728644
  89.3 31.1 %slice-start = ((s8[5242880]{0:T(1024)(128)(4,1)}), s8[1048576]{0:T(1024)(128)(4,1)S(1)}, s32[]{:S(2)}) async-start(s8[5242880]{0:T(1024)(128)(4,1)} %bitcast.65), calls=%async_computation.1 | async-start | bytes 2097152
  108.1 5.7 %copy-start.3 = (bf16[2560,768]{1,0:T(8,128)(2,1)S(1)}, bf16[2560,768]{1,0:T(8,128)(2,1)}, u32[]{:S(2)}) copy-start(bf16[2560,768]{1,0:T(8,128)(2,1)} %param.17) | copy-start | bytes 11796484
  108.1 12.3 %slice-start.1 = ((s8[5242880]{0:T(1024)(128)(4,1)}), s8[4194304]{0:T(1024)(128)(4,1)S(1)}, s32[]{:S(2)}) async-start(s8[5242880]{0:T(1024)(128)(4,1)} %bitcast.65), calls=%async_computation.2 | async-start | bytes 8388608
  113.8 6.5 %copy-start.4 = (bf16[2560,768]{1,0:T(8,128)(2,1)S(1)}, bf16[2560,768]{1,0:T(8,128)(2,1)}, u32[]{:S(2)}) copy-start(bf16[2560,768]{1,0:T(8,128)(2,1)} %param.18) | copy-start | bytes 11796484
  120.4 4.5 %copy-start.2 = (bf16[768,2560]{1,0:T(8,128)(2,1)S(1)}, bf16[768,2560]{1,0:T(8,128)(2,1)}, u32[]{:S(2)}) copy-start(bf16[768,2560]{1,0:T(8,128)(2,1)} %param.19) | copy-start | bytes 11796484
  124.9 0.9 copy-start.5
Sparse Core Ops, SparseCore 0:
  28.6 41.3 all-gather.1

commit v2 on v1

--- a/solution.py
+++ b/solution.py
@@ -141,11 +141,18 @@
     tokens = rows * dp
     table = jnp.concatenate([routes.astype(F32), route_weights], axis=1)
     table = lax.all_gather(table, "dp", axis=0, tiled=True)
-    gathered = lax.all_gather(hidden, "mp", axis=1, tiled=True)
+    both = dp == 8 and mp == 4
+    if both:
+        gathered = lax.all_gather(hidden, ("dp", "mp"), axis=0, tiled=False)
+        gathered = gathered.reshape(dp, mp, rows, hidden.shape[1])
+        gathered = jnp.transpose(gathered, (0, 2, 1, 3)).reshape(tokens, mp * hidden.shape[1])
+    else:
+        gathered = lax.all_gather(hidden, "mp", axis=1, tiled=True)
     values = gathered.astype(F32)
     factor = lax.rsqrt(jnp.mean(values * values, axis=-1, keepdims=True) + 1e-06)
-    own_normed = (values * factor * norm_gain.astype(F32)).astype(BF16)
-    normed = lax.all_gather(own_normed, "dp", axis=0, tiled=True)
+    normed = (values * factor * norm_gain.astype(F32)).astype(BF16)
+    if not both:
+        normed = lax.all_gather(normed, "dp", axis=0, tiled=True)
     width = normed.shape[1]
 
     all_routes = table[:, :top].reshape(dp, rows, top)
@@ -196,7 +203,7 @@
     is_own = (jnp.arange(dp) == me)[:, None, None]
     total = routed + adapted.reshape(dp, rows, width) + jnp.where(is_own, own_shared[None], 0.0)
     total = total.astype(BF16)
-    if dp == 8 and mp == 4:
+    if both:
         return reduce_scatter(total, mp)
     total = total.reshape(tokens, width)
     part = lax.psum_scatter(total, "dp", scatter_dimension=0, tiled=True)

time: 178 us -> 223 us (1.25)
  waiting for transfers between devices: 27.8 us -> 56 us
  local copies, waits for them, and re-layouts: 6.74 us -> 27 us
  blocking collectives: 29.1 us -> 10.5 us
  matrix products: 49.5 us -> 60.2 us
  other arithmetic: 8.73 us -> 12.8 us
    all_gather x1, waiting for transfers between devices: 27.8 us -> 55.3 us  [body(): gathered = lax.all_gather(hidden, ('dp', 'mp'), axis=0, tiled=False)]
    convert_element_type x0 -> x2, local copies, waits for them, and re-layouts: none -> 21.1 us  [body(): values = gathered.astype(F32)]
    all_gather x1 -> x0, blocking collectives: 19.8 us -> none  [body(): gathered = lax.all_gather(hidden, 'mp', axis=1, tiled=True)]
    unnamed x1, matrix products: 3.99 us -> 9.57 us
    dot_general x1, matrix products: 4.47 us -> 7.87 us  [body(): shared_pre = jnp.dot(normed, shared_up, preferred_element_type=F32)]
    reduce_sum x1 -> x2, other arithmetic: 0.22 us -> 3.6 us  [body(): jnp.mean(values * values, axis=-1, keepdims=True) + 1e-06]
    convert_element_type x1, local copies, waits for them, and re-layouts: 2.82 us -> 0.35 us  [body(): slots_in = slots_in.astype(BF16).reshape(experts, dp * cap, width)]
    unnamed x17 -> x19, local copies, waits for them, and re-layouts: 3.16 us -> 4.83 us
  transfers between devices with their start and end apart: 1 -> 1, of which waited for: 1 -> 1; matrix products, arithmetic and copies ran while one was open for 3% -> 2% of each run, Pallas kernels for 0% -> 0%
where the time goes in v2:
time: 223 us; the launch traced here: 222 us
  matrix products  60.2 us (27%)
  waiting for transfers between devices  56 us (25%)
  Pallas kernels  41.7 us (19%)
  local copies, waits for them, and re-layouts  27 us (12%)
  between operations  13.6 us (6%)
  other arithmetic  12.8 us (6%)
  blocking collectives  10.5 us (5%)
    all_gather x1, waiting for transfers between devices, body(): gathered = lax.all_gather(hidden, ('dp', 'mp'), axis=0, tiled=False)  55.3 us
    pallas_call x1, Pallas kernels, reduce_scatter(): pl.pallas_call(functools.partial(scatter_kernel, mp), out_shape=jax.Shape...  41.7 us
    convert_element_type x2, local copies, waits for them, and re-layouts, body(): values = gathered.astype(F32)  21.1 us
    dot_general x1, matrix products, body(): jnp.einsum('jcf,jfd->jcd', inner, expert_down, preferred_element_type=F32)  18.7 us
    all_gather x1, blocking collectives, body(): table = lax.all_gather(table, 'dp', axis=0, tiled=True)  10.5 us
    unnamed x1, matrix products  9.57 us
    dot_general x1, matrix products, body(): shared_lin = jnp.dot(normed, shared_gate, preferred_element_type=F32)  8.31 us
    dot_general x1, matrix products, body(): shared_pre = jnp.dot(normed, shared_up, preferred_element_type=F32)  7.87 us
  transfers between devices with their start and end apart: 1, of which 1 were waited for; matrix products, arithmetic and copies ran while one was open for 2% of the time, Pallas kernels for 0%

profile of v2, /device:TPU:0, one launch (start us, length us, event | category | flops | bytes accessed | tf_op | source)
XLA Modules:
  0.0 221.9 jit_solution(10324773408780615202)
XLA Ops:
  6.5 0.0 copy-start
  6.5 0.0 all-gather.3.cloned.1.call-start
  6.5 0.7 all-gather.3.cloned.1.call-update
  7.3 0.7 convert_element_type.73
  8.0 0.7 convert_element_type.82
  8.6 0.7 copy.42
  9.4 0.1 reduce-window.8
  9.5 0.1 reduce.5
  9.6 0.7 sub.9
  10.3 0.7 pad_maximum_fusion
  11.0 10.5 %all_gather.9 = f32[1024,12]{0,1:T(8,128)S(1)} all-gather(f32[128,12]{0,1:T(8,128)S(1)} %pad_maximum_fusion), channel_id=1, replica_groups=mesh['dp'=8,'mp'=4] {'dp'}, dimensions={0}, use_global_device_ids=true | all-gather | bytes 55296 | tf_op jit(solution)/shard_map/all_gather | solution.py:143
  21.5 0.8 select_reduce_fusion.2
  22.3 0.1 fusion.16
  22.4 0.1 select_reduce_fusion.1
  22.5 0.1 fusion.12
  22.6 0.2 select_reduce_fusion
  22.9 0.1 iota_compare_fusion
  23.0 55.3 %all-gather.3.cloned.1.call-done = bf16[4096,640]{1,0:T(8,128)(2,1)} async-done(((bf16[128,640]{1,0:T(8,128)(2,1)}), bf16[4096,640]{1,0:T(8,128)(2,1)}) %all-gather.3.cloned.1.call-update) | async-done | bytes 5242896 | tf_op jit(solution)/shard_map/all_gather | solution.py:146
  78.2 3.6 %multiply_reduce_fusion = f32[4096]{0:T(1024)S(1)} fusion(bf16[4096,640]{1,0:T(8,128)(2,1)} %all-gather.3.cloned.1.call-done), kind=kLoop, calls=%fused_computation.8 | loop fusion | flops 7860224 | bytes 5259264 | tf_op jit(solution)/shard_map/reduce_sum | solution.py:152
  81.9 9.6 %copy.36 = f32[8,4,128,640]{2,0,3,1:T(8,128)} copy(bf16[8,4,128,640]{3,2,1,0:T(8,128)(2,1)} %bitcast.85) | data formatting | bytes 15728640 | tf_op jit(solution)/shard_map/convert_element_type | solution.py:151
  91.5 11.5 %copy.38 = f32[8,128,2560]{2,1,0:T(8,128)} copy(f32[8,128,2560]{1,0,2:T(8,128)} %bitcast.79) | data formatting | bytes 20971520 | tf_op jit(solution)/shard_map/convert_element_type | solution.py:151
  103.0 9.6 %fusion.5 = f32[8,2560,128]{1,2,0} fusion(pred[8,128,128]{1,2,0:T(8,128)(4,1)S(1)} %bitcast.86, f32[8,128,2560]{2,1,0:T(8,128)} %copy.38, f32[2560]{0:T(1024)S(1)} %convert_element_type.82, f32[8,128]{1,0:T(8,128)S(1)} %get-tuple-element.10), kind=kOutput, calls=%fused_computation.10 | convolution fusion | flops 678952960 | bytes 21116928
  112.5 0.0 slice-start.1
  112.5 4.9 %convert_bitcast_fusion = bf16[8,8,16,2560]{3,2,0,1:T(8,128)(2,1)S(1)} fusion(f32[8,2560,8,16]{1,3,2,0:T(8,128)} %bitcast.84), kind=kLoop, calls=%fused_computation.13 | loop fusion | flops 2621440 | bytes 15728640 | tf_op jit(solution)/shard_map/convert_element_type | solution.py:172
  117.5 0.0 slice-start.2
  117.5 0.3 copy.39
  117.8 0.0 copy-start.1
  117.9 0.0 slice-done
  117.9 0.5 slice-done.1
  118.4 3.4 %slice-done.2 = s8[4194304]{0:T(1024)(128)(4,1)S(1)} async-done(((s8[10485760]{0:T(1024)(128)(4,1)}), s8[4194304]{0:T(1024)(128)(4,1)S(1)}, s32[]{:S(2)}) %slice-start.2) | async-done | bytes 4194328
  121.8 0.0 copy-start.4
  121.8 8.3 %fusion.26 = f32[1024,768]{1,0:T(8,128)S(1)} fusion(bf16[2560,768]{1,0:T(8,128)(2,1)} %param.17, f32[320,8,8,128]{3,2,1,0:T(8,128)S(1)} %bitcast.82, f32[2560]{0:T(1024)S(1)} %convert_element_type.82, f32[1024]{0:T(1024)S(1)} %get-tuple-element.9), kind=kOutput, calls=%fused_computation.53 | convolution fusion | flops 4034396160 | bytes 17577984 | tf_op jit(solution)/shard_map/dot_general | solution.py:180
  130.1 0.0 copy-done.4
  130.1 7.9 %multiply_convert_fusion.2 = bf16[1024,768]{1,0:T(8,128)(2,1)} fusion(f32[1024,768]{1,0:T(8,128)S(1)} %fusion.26, bf16[2560,768]{1,0:T(8,128)(2,1)S(1)} %copy-done.4, f32[320,8,8,128]{3,2,1,0:T(8,128)S(1)} %bitcast.83, f32[2560]{0:T(1024)S(1)} %convert_element_type.82, f32[1024]{0:T(1024)S(1)} %get-tuple-element.9), kind=kOutput, calls=%fused_computation.16 | convolution fusion | flops 4039114752 | bytes 19150848 | tf_op jit(solution)/shard_map/dot_general | solution.py:181
  138.0 0.0 copy-done.1
  138.0 7.1 %fusion.28 = f32[8,128,384]{2,1,0:T(8,128)S(1)} fusion(bf16[8,128,2560]{2,1,0:T(8,128)(2,1)S(1)} %bitcast.77, bf16[8,2560,384]{2,1,0:T(8,128)(2,1)} %param.20), kind=kOutput, calls=%fused_computation.54 | convolution fusion | flops 2013265920 | bytes 22544384 | tf_op jit(solution)/shard_map/jcd,jdf->jcf/dot_general | solution.py:173
  145.1 18.7 %fusion.29 = f32[8,128,2560]{2,1,0:T(8,128)} fusion(bf16[8,384,2560]{2,1,0:T(8,128)(2,1)} %param.22, f32[8,128,384]{2,1,0:T(8,128)S(1)} %fusion.28, bf16[8,128,2560]{2,1,0:T(8,128)(2,1)} %bitcast.78, bf16[8,2560,384]{2,1,0:T(8,128)(2,1)} %param.21), kind=kOutput, calls=%fused_computation.55 | convolution fusion | flops 4028891136 | bytes 48758784 | tf_op jit(solution)/shard_map/jcf,jfd->jcd/dot_general | solution.py:176
  163.8 5.7 %fusion.6 = f32[8,128,2560,1]{2,1,3,0:T(8,128)S(1)} fusion(f32[8,8,16,2560]{3,2,1,0:T(8,128)} %bitcast.76, f32[8,8,16]{2,0,1:T(8,128)S(1)} %bitcast.88, f32[8,128,8]{1,2,0:T(8,128)S(1)} %fusion.12), kind=kOutput, calls=%fused_computation.11 | convolution fusion | flops 676462592 | bytes 21008384 | tf_op jit(solution)/shard_map/stjc,jscd->std/dot_general | solution.py:178
  169.6 0.0 copy-done.2
  169.6 0.0 copy-done.3
  169.6 0.0 copy-start.5
  169.6 0.7 fusion.17
  170.3 0.2 copy-done.5
  170.5 0.6 fusion.11
  171.1 0.0 copy-done
  171.1 1.5 fusion.3.total
  172.6 41.7 %shard_map.145 = bf16[128,640]{1,0:T(8,128)(2,1)S(1)} custom-call(bf16[8,128,2560]{2,1,0:T(8,128)(2,1)S(1)} %fusion.3.total), custom_call_target="tpu_custom_call" | custom-call | tf_op jit(solution)/shard_map/pallas_call | solution.py:100
  214.4 0.7 copy.54
  (10 shorter events, 0.0 us)
Async XLA Ops:
  6.5 164.6 %copy-start = (bf16[8,16,2560]{2,1,0:T(8,128)(2,1)S(1)}, bf16[8,16,2560]{2,1,0:T(8,128)(2,1)}, u32[]{:S(2)}) copy-start(bf16[8,16,2560]{2,1,0:T(8,128)(2,1)} %param.24) | copy-start | bytes 1966084
  6.5 71.7 %all-gather.3.cloned.1.call-start = ((), (), s32[]{:S(2)}) async-start(), calls=%async_computation | async-start | bytes 5406720 | tf_op jit(solution)/shard_map/all_gather | solution.py:146
  112.5 5.3 %slice-start = ((s8[10485760]{0:T(1024)(128)(4,1)}), s8[4194304]{0:T(1024)(128)(4,1)S(1)}, s32[]{:S(2)}) async-start(s8[10485760]{0:T(1024)(128)(4,1)} %bitcast.80), calls=%async_computation.1 | async-start | bytes 8388608
  112.5 5.8 %slice-start.1 = ((s8[10485760]{0:T(1024)(128)(4,1)}), s8[2097152]{0:T(1024)(128)(4,1)S(1)}, s32[]{:S(2)}) async-start(s8[10485760]{0:T(1024)(128)(4,1)} %bitcast.80), calls=%async_computation.2 | async-start | bytes 4194304
  117.5 4.3 %slice-start.2 = ((s8[10485760]{0:T(1024)(128)(4,1)}), s8[4194304]{0:T(1024)(128)(4,1)S(1)}, s32[]{:S(2)}) async-start(s8[10485760]{0:T(1024)(128)(4,1)} %bitcast.80), calls=%async_computation.3 | async-start | bytes 8388608
  117.8 20.1 %copy-start.1 = (bf16[8,8,16,2560]{3,2,1,0:T(8,128)(2,1)}, bf16[8,8,16,2560]{3,2,1,0:T(8,128)(2,1)S(1)}, u32[]{:S(2)}) copy-start(bf16[8,8,16,2560]{3,2,1,0:T(8,128)(2,1)S(1)} %copy.39) | copy-start | bytes 15728644
  121.8 8.3 %copy-start.4 = (bf16[2560,768]{1,0:T(8,128)(2,1)S(1)}, bf16[2560,768]{1,0:T(8,128)(2,1)}, u32[]{:S(2)}) copy-start(bf16[2560,768]{1,0:T(8,128)(2,1)} %param.18) | copy-start | bytes 11796484
  163.8 5.7 %copy-start.2 = (bf16[768,2560]{1,0:T(8,128)(2,1)S(1)}, bf16[768,2560]{1,0:T(8,128)(2,1)}, u32[]{:S(2)}) copy-start(bf16[768,2560]{1,0:T(8,128)(2,1)} %param.19) | copy-start | bytes 11796484
  163.8 5.7 %copy-start.3 = (bf16[1024,768]{1,0:T(8,128)(2,1)S(1)}, bf16[1024,768]{1,0:T(8,128)(2,1)}, u32[]{:S(2)}) copy-start(bf16[1024,768]{1,0:T(8,128)(2,1)} %multiply_convert_fusion.2) | copy-start | bytes 4718596
  169.6 0.9 copy-start.5
Sparse Core Ops, SparseCore 0:
  10.2 68.0 all-gather.2
